TPU v7x, 512 devices: a whole 4x4x16 slice. The times are simulated.
512 devices in a mesh: group: 4 (over z_hi), dp: 32 (over y, z_lo, core), tensor: 4 (over x).
Axes of the slice: x: 4, y: 4, z: 16 (z_hi: 4, z_lo: 4; z = z_hi * 4 + z_lo), core: 2. Of those that a mesh axis runs over, the one named last changes fastest.
Arguments:
- queries: bfloat16 [16384, 4096], P(('group', 'dp'), 'tensor'), may hold values from -16 to 16
- span_state: bfloat16 [16384, 4096], P(('group', 'dp'), 'tensor'), may hold values from -6 to 6
- neigh_state: bfloat16 [65536, 4096], P(('group', 'dp'), 'tensor'), may hold values from -24 to 24
- counts: int32 [4, 64], P('group'), may hold values from 1 to 2
- norm_gain: float32 [4096], P('tensor'), may hold values from 0.5 to 1.5
- head_gate: float32 [32], P('tensor'), may hold values from 0.3 to 1.5
- out_grad: bfloat16 [16384, 4096], P(('group', 'dp'), 'tensor'), may hold values from -6 to 6
Outputs:
- cross_output: bfloat16 [16384, 4096], P(('group', 'dp'), 'tensor')
- query_grad: bfloat16 [16384, 4096], P(('group', 'dp'), 'tensor')
- span_grad: bfloat16 [16384, 4096], P(('group', 'dp'), 'tensor')
- neighbour_grad: bfloat16 [65536, 4096], P(('group', 'dp'), 'tensor')
- gate_grad: float32 [32], P('tensor')
Inputs may be any that keep to these rules, and one draw needn't show every extreme that they name: Slot j of span c holds a retrieved neighbour exactly when j < counts[c].
All inputs are finite; a program needn't handle non-finite values.
Results may differ from a plain program's by a relative error of at most 0.0095.
The roundings to bfloat16 on the way count: a program that leaves them out, or rounds other values in their place, can miss the bound.
Values may be sent and summed in bfloat16 or wider, within the bound.
No kernel may reach another device: no remote copies, remote signals or barrier semaphores. Data moves between devices by JAX's collectives and lax.ppermute only.
A program may use at most 64 MiB of HBM per device.

v0:
```python
import math
import jax
import jax.numpy as jnp
from jax import lax
from jax.sharding import PartitionSpec as P

CH = 64
NB = 2
NL = 128
epsilon = 1e-05
masked_score = -1e30


def shifted(value, axis, steps):
    count = lax.axis_size(axis)
    leading, last = (max(0, -steps), min(count, count - steps))
    return lax.ppermute(value, axis, [(source, source + steps) for source in range(leading, last)])


def product(form, left, right):
    return jnp.einsum(form, left, right, preferred_element_type=jnp.float32)


def encoder_forward(normed, neighbours, contexts):
    slot_count = normed.shape[1]
    spread = jnp.broadcast_to(
        contexts[:, None], (contexts.shape[0], slot_count) + contexts.shape[1:]
    )
    all_keys = jnp.concatenate([normed, spread], axis=2)
    scores = product("cjqhd,cjkhd->cjhqk", normed, all_keys) / normed.shape[-1]
    powers = jnp.exp(scores)
    weights = powers / jnp.sum(powers, axis=-1, keepdims=True)
    rounded = weights.astype(jnp.bfloat16)
    mixture = product("cjhqk,cjkhd->cjqhd", rounded, all_keys)
    encoded = (neighbours.astype(jnp.float32) + mixture).astype(jnp.bfloat16)
    return (encoded, (all_keys, weights, rounded, mixture))


def encoder_backward(grad_encoded, normed, saved):
    all_keys, weights, rounded, mixture = saved
    grad_rounded = grad_encoded.astype(jnp.bfloat16)
    grad_weights = product("cjqhd,cjkhd->cjhqk", grad_rounded, all_keys)
    offset = jnp.moveaxis(jnp.sum(grad_encoded * mixture, axis=-1), -1, 2)[..., None]
    score_grad = (weights * (grad_weights - offset) / normed.shape[-1]).astype(jnp.bfloat16)
    normed_grad = product("cjhqk,cjkhd->cjqhd", score_grad, all_keys)
    key_grad = product("cjhqk,cjqhd->cjkhd", score_grad, normed) + product(
        "cjhqk,cjqhd->cjkhd", rounded, grad_rounded
    )
    length = normed.shape[2]
    normed_grad = normed_grad + key_grad[:, :, :length]
    context_grad = jnp.sum(key_grad[:, :, length:], axis=1)
    return (normed_grad, context_grad)


def cross_attend(blocks, grad_blocks, keys, usable, present, gate_tanh):
    scale = 1.0 / math.sqrt(blocks.shape[-1])
    scores = product("brhd,bmhd->bhrm", blocks, keys) * scale
    scores = jnp.where(usable[:, None, None, :], scores, masked_score)
    highest = jnp.max(scores, axis=-1, keepdims=True)
    powers = jnp.exp(scores - highest)
    weights = powers / jnp.sum(powers, axis=-1, keepdims=True)
    rounded = weights.astype(jnp.bfloat16)
    attended = product("bhrm,bmhd->brhd", rounded, keys)
    present_mask = present[:, None, None, None]
    attended = jnp.where(present_mask, attended, 0.0)
    output = (gate_tanh[:, None] * attended).astype(jnp.bfloat16)
    grad_output = grad_blocks.astype(jnp.float32)
    gate_term = jnp.sum(grad_output * attended, axis=(0, 1, 3))
    att_grad = jnp.where(present_mask, gate_tanh[:, None] * grad_output, 0.0)
    grad_rounded = att_grad.astype(jnp.bfloat16)
    grad_weights = product("brhd,bmhd->bhrm", grad_rounded, keys)
    offset = jnp.moveaxis(jnp.sum(att_grad * attended, axis=-1), -1, 1)[..., None]
    score_grad = (weights * (grad_weights - offset) * scale).astype(jnp.bfloat16)
    query_grad = product("bhrm,bmhd->brhd", score_grad, keys).astype(jnp.bfloat16)
    key_grad = product("bhrm,brhd->bmhd", score_grad, blocks) + product(
        "bhrm,brhd->bmhd", rounded, grad_rounded
    )
    return (output, query_grad, key_grad, gate_term)


def shards(queries, span_state, neigh_state, counts, norm_gain, head_gate, out_grad):
    head_count = head_gate.shape[0]
    local_width = queries.shape[1]
    head_dim = local_width // head_count
    row_count = queries.shape[0]
    span_count = row_count // CH
    seq_spans = counts.shape[1]
    lead = CH - 1

    def blockify(matrix):
        return matrix.reshape(-1, CH, head_count, head_dim)

    neighbours = neigh_state.reshape(span_count, NB, NL, head_count, head_dim)
    contexts = span_state.reshape(span_count, CH, head_count, head_dim)
    gains = norm_gain.reshape(head_count, head_dim)
    floats = neighbours.astype(jnp.float32)
    square_sum = lax.psum(jnp.sum(floats * floats, axis=(3, 4)), "tensor")
    full_width = lax.axis_size("tensor") * local_width
    inverse = lax.rsqrt(square_sum / full_width + epsilon)[..., None, None]
    scaled = floats * inverse
    normed = (scaled * gains).astype(jnp.bfloat16)
    encoded, saved = encoder_forward(normed, neighbours, contexts)
    line_index = lax.axis_index("dp")
    first_span = line_index * span_count
    flat_counts = counts.reshape(-1)
    own_counts = lax.dynamic_slice_in_dim(flat_counts, first_span, span_count)
    gate_tanh = jnp.tanh(head_gate)
    usable = jnp.repeat(jnp.arange(NB)[None, :] < own_counts[:, None], NL, axis=1)
    present = own_counts > 0
    keys = encoded.reshape(span_count, NB * NL, head_count, head_dim)
    kept = row_count - lead
    padding = jnp.zeros((lead, local_width), jnp.bfloat16)
    blocks = blockify(jnp.concatenate([queries[lead:], padding], axis=0))
    grad_blocks = blockify(jnp.concatenate([out_grad[lead:], padding], axis=0))
    earlier_keys = shifted(keys[span_count - 1], "dp", 1)
    earlier_count = lax.dynamic_index_in_dim(
        flat_counts, jnp.maximum(first_span - 1, 0), keepdims=False
    )
    earlier_present = jnp.logical_and(first_span % seq_spans > 0, earlier_count > 0)
    earlier_usable = jnp.repeat(jnp.arange(NB) < earlier_count, NL)
    front_row = jnp.zeros((1, local_width), jnp.bfloat16)
    first_block = blockify(jnp.concatenate([front_row, queries[:lead]], axis=0))
    first_grad = blockify(jnp.concatenate([front_row, out_grad[:lead]], axis=0))
    front_out, front_query, front_keys, front_term = cross_attend(
        first_block,
        first_grad,
        earlier_keys[None],
        earlier_usable[None],
        earlier_present[None],
        gate_tanh,
    )
    local_out, local_query, key_grad, local_term = cross_attend(
        blocks, grad_blocks, keys, usable, present, gate_tanh
    )
    returned = shifted(front_keys[0].astype(jnp.bfloat16), "dp", -1).astype(jnp.float32)
    key_grad = key_grad.at[span_count - 1].add(returned)
    cross_output = jnp.concatenate(
        [front_out.reshape(CH, local_width)[1:], local_out.reshape(row_count, local_width)[:kept]],
        axis=0,
    )
    query_grad = jnp.concatenate(
        [
            front_query.reshape(CH, local_width)[1:],
            local_query.reshape(row_count, local_width)[:kept],
        ],
        axis=0,
    )
    gate_terms = front_term + local_term
    grad_encoded = key_grad.reshape(span_count, NB, NL, head_count, head_dim)
    normed_grad, context_grad = encoder_backward(grad_encoded, normed, saved)
    gain_grad = normed_grad * gains
    projection = lax.psum(jnp.sum(gain_grad * scaled, axis=(3, 4)), "tensor") / full_width
    neighbour_grad = grad_encoded + inverse * (gain_grad - scaled * projection[..., None, None])
    total_tokens = lax.axis_size("group") * lax.axis_size("dp") * row_count
    summed = lax.psum(gate_terms, ("group", "dp"))
    gate_grad = (1.0 - gate_tanh * gate_tanh) * summed / math.sqrt(total_tokens)
    return (
        cross_output,
        query_grad,
        context_grad.reshape(row_count, local_width).astype(jnp.bfloat16),
        neighbour_grad.reshape(-1, local_width).astype(jnp.bfloat16),
        gate_grad,
    )


def solution(mesh):
    return jax.shard_map(
        shards,
        mesh=mesh,
        in_specs=(
            P(("group", "dp"), "tensor"),
            P(("group", "dp"), "tensor"),
            P(("group", "dp"), "tensor"),
            P("group", None),
            P("tensor"),
            P("tensor"),
            P(("group", "dp"), "tensor"),
        ),
        out_specs=(
            P(("group", "dp"), "tensor"),
            P(("group", "dp"), "tensor"),
            P(("group", "dp"), "tensor"),
            P(("group", "dp"), "tensor"),
            P("tensor"),
        ),
        check_vma=False,
    )
```

profile of v0, /device:TPU:2, one launch (start us, length us, event | category | flops | bytes accessed | tf_op | source)
XLA Modules:
  0.0 361.5 jit_solution(13486729681499176493)
XLA Ops:
  0.6 1.5 fusion.4
  2.2 2.8 convert_bitcast_fusion
  5.0 13.6 %psum.21 = f32[2,2,128]{2,1,0:T(2,128)S(1)} all-reduce(f32[2,2,128]{2,1,0:T(2,128)S(1)} %bitcast.184), channel_id=1, replica_groups=mesh['group'=4,'dp'=32,'tensor'=4] {'tensor'}, use_global_device_ids=true, to_apply=%region_1.0 | all-reduce | flops 512 | bytes 4096 | tf_op jit(solution)/shard_map/psum | solution.py:97
  18.7 2.1 copy.109
  22.5 2.4 fusion.6
  27.2 2.1 collective-permute-start
  32.5 1.9 copy.82
  40.4 5.0 %multiply_reduce_fusion.1 = (f32[8]{0:T(128)}, f32[2,64,8]{1,2,0:T(8,128)}, bf16[2,64,8,128]{3,1,2,0:T(8,128)(2,1)}) fusion(f32[2,64,8,128]{3,2,1,0:T(8,128)} %bitcast.171, f32[8]{0:T(128)} %tanh.3, pred[2]{0:T(512)(128)(4,1)} %get-tuple-element.21, bf16[2,256,8,128]{3,2,1,0:T(8,128)(2,1)S(1)} %bitcast.155, f32[2,8,64]{2,1,0:T(8,128)S(1)} %get-tuple-element.30, ...), kind=kOutput, calls=%fused_computation.63 | convolution fusion | flops 69075192 | bytes 2891842 | tf_op jit(solution)/shard_map/bhrm,bmhd->brhd/dot_general | solution.py:21
  45.4 2.0 fusion.13
  48.4 1.9 fusion.41
  52.5 6.2 %add_bitcast_fusion.1 = f32[2,256,8,128]{1,3,2,0:T(8,128)} fusion(f32[2,8,128,256]{3,2,1,0:T(8,128)} %fusion.41, f32[2,64,8,128]{3,2,1,0:T(8,128)} %bitcast.173, f32[8]{0:T(128)S(1)} %copy-done.14, pred[2]{0:T(512)(128)(4,1)S(1)} %copy-done.16, f32[2,8,64]{2,1,0:T(8,128)S(1)} %get-tuple-element.30, f32[2,8,64,256]{3,2,1,0:T(8,128)} %copy-done.3), kind=kOutput, calls=%fused_computation.18 | convolution fusion | flops 68814080 | bytes 5771298 | tf_op jit(solution)/shard_map/bhrm,brhd->bmhd/dot_general | solution.py:21
  58.6 1.4 fusion.21
  60.9 2.8 multiply_reduce_fusion.3
  63.7 1.6 fusion.24
  65.3 1.3 fusion.45
  66.7 3.4 fusion.17
  72.4 254.7 %psum.23 = f32[8]{0:T(128)S(1)} all-reduce(f32[8]{0:T(128)S(1)} %add.79), channel_id=1, replica_groups=mesh['group'=4,'dp'=32,'tensor'=4] {'group','dp'}, use_global_device_ids=true, to_apply=%region_15.16 | all-reduce | flops 8 | bytes 64 | tf_op jit(solution)/shard_map/psum | solution.py:155
  330.2 2.3 fusion.28
  332.5 3.0 copy.96
  335.5 1.9 convert_element_type.156
  337.7 2.3 fusion.7
  342.8 2.6 multiply_reduce_fusion
  346.3 10.1 %psum.22 = f32[2,2,128]{2,1,0:T(2,128)S(1)} all-reduce(f32[2,2,128]{2,1,0:T(2,128)S(1)} %get-tuple-element.35), channel_id=1, replica_groups=mesh['group'=4,'dp'=32,'tensor'=4] {'tensor'}, use_global_device_ids=true, to_apply=%region_12.13 | all-reduce | flops 512 | bytes 4096 | tf_op jit(solution)/shard_map/psum | solution.py:152
  356.5 3.1 add_convert_fusion
  (112 shorter events, 27.7 us)
Async XLA Ops:
  0.6 18.0 %copy-start.10 = (bf16[128,1024]{1,0:T(8,128)(2,1)S(1)}, bf16[128,1024]{1,0:T(8,128)(2,1)}, u32[]{:S(2)}) copy-start(bf16[128,1024]{1,0:T(8,128)(2,1)} %param.10) | copy-start | bytes 786436
  18.7 2.1 copy-start.13
  22.4 2.6 copy-start.21
  22.4 2.6 copy-start.23
  24.9 4.4 %copy-start.15 = (s32[1,64]{1,0:T(1,128)S(1)}, s32[1,64]{1,0:T(1,128)}, u32[]{:S(2)}) copy-start(s32[1,64]{1,0:T(1,128)} %param.12) | copy-start | bytes 772
  24.9 6.8 %copy-start.9 = (bf16[128,1024]{1,0:T(8,128)(2,1)S(1)}, bf16[128,1024]{1,0:T(8,128)(2,1)}, u32[]{:S(2)}) copy-start(bf16[128,1024]{1,0:T(8,128)(2,1)} %param.9) | copy-start | bytes 786436
  25.0 6.9 %copy-start.8 = (bf16[128,1024]{1,0:T(8,128)(2,1)S(1)}, bf16[128,1024]{1,0:T(8,128)(2,1)}, u32[]{:S(2)}) copy-start(bf16[128,1024]{1,0:T(8,128)(2,1)} %param.15) | copy-start | bytes 786436
  26.3 8.2 %copy-start.17 = (f32[8]{0:T(128)S(1)}, f32[8]{0:T(128)}, u32[]{:S(2)}) copy-start(f32[8]{0:T(128)} %param.14) | copy-start | bytes 100
  27.2 31.4 %collective-permute-start = (bf16[256,8,128]{2,0,1:T(8,128)(2,1)}, bf16[256,8,128]{2,0,1:T(8,128)(2,1)}, u32[]{:S(2)}, u32[]{:S(2)}) collective-permute-start(bf16[256,8,128]{2,0,1:T(8,128)(2,1)} %copy.79), channel_id=1, source_target_pairs={{0,4},{4,8},{8,12},{12,16},{16,20},{20,24},{24,28},{28,32},{32,36}... | collective-permute-start | bytes 1572872 | tf_op jit(solution)/shard_map/ppermute | solution.py:17
  48.4 1.9 slice-start
  48.4 3.4 copy-start.7
  50.3 1.8 copy-start.12
  50.3 2.1 copy-start.20
  50.3 2.1 copy-start.14
  50.3 2.1 copy-start.16
  58.6 2.3 copy-start.11
  65.3 6.0 %copy-start.19 = (f32[8]{0:T(128)S(1)}, f32[8]{0:T(128)}, u32[]{:S(2)}) copy-start(f32[8]{0:T(128)} %get-tuple-element.17) | copy-start | bytes 100
  70.1 260.1 %collective-permute-start.1 = (bf16[256,8,128]{0,2,1:T(8,128)(2,1)}, bf16[256,8,128]{0,2,1:T(8,128)(2,1)S(1)}, u32[]{:S(2)}, u32[]{:S(2)}) collective-permute-start(bf16[256,8,128]{0,2,1:T(8,128)(2,1)} %fusion.17), channel_id=1, source_target_pairs={{4,0},{8,4},{12,8},{16,12},{20,16},{24,20},{28,24},{32,28},{36,32}... | collective-permute-start | bytes 1572872 | tf_op jit(solution)/shard_map/ppermute | solution.py:17
  71.4 258.3 %copy-start.18 = (f32[8]{0:T(128)S(1)}, f32[8]{0:T(128)}, u32[]{:S(2)}) copy-start(f32[8]{0:T(128)} %param.14) | copy-start | bytes 100
  335.5 2.2 copy-start
  335.5 4.6 %copy-start.22 = (f32[2,2,8,128,192]{3,4,2,1,0:T(8,128)S(1)}, f32[2,2,8,128,192]{3,4,2,1,0:T(8,128)}, u32[]{:S(2)}) copy-start(f32[2,2,8,128,192]{3,4,2,1,0:T(8,128)} %copy-done.21) | copy-start | bytes 9437188
  337.7 2.3 copy-start.2
  337.7 2.4 copy-start.6
  337.7 2.4 copy-start.24
  (4 other events, 3.9 us)
where the time goes:
time: 362 us
  blocking collectives  278 us (77%)
  matrix products  36.8 us (10%)
  other arithmetic  22.9 us (6%)
  local copies, waits for them, and re-layouts  18.3 us (5%)
    psum x1, blocking collectives, shards(): summed = lax.psum(gate_terms, ('group', 'dp'))  255 us
    dot_general x18, matrix products, product(): return jnp.einsum(form, left, right, preferred_element_type=jnp.float32)  36.8 us
    psum x1, blocking collectives, shards(): square_sum = lax.psum(jnp.sum(floats * floats, axis=(3, 4)), 'tensor')  13.6 us
    psum x1, blocking collectives, shards(): lax.psum(jnp.sum(gain_grad * scaled, axis=(3, 4)), 'tensor') / full_width  10.1 us
    unnamed x66, local copies, waits for them, and re-layouts  8.57 us
  transfers between devices with their start and end apart: 2, of which 0 were waited for; matrix products, arithmetic and copies ran while one was open for 9% of the time, Pallas kernels for 0%

commit v1 on v0

--- a/solution.py
+++ b/solution.py
@@ -9,6 +9,11 @@
 NL = 128
 epsilon = 1e-05
 masked_score = -1e30
+
+
+def axis_by_axis(value_2, inner_axis, outer_axis):
+    inner = lax.psum(value_2, inner_axis)
+    return lax.psum(inner, outer_axis)
 
 
 def shifted(value, axis, steps):
@@ -152,7 +157,7 @@
     projection = lax.psum(jnp.sum(gain_grad * scaled, axis=(3, 4)), "tensor") / full_width
     neighbour_grad = grad_encoded + inverse * (gain_grad - scaled * projection[..., None, None])
     total_tokens = lax.axis_size("group") * lax.axis_size("dp") * row_count
-    summed = lax.psum(gate_terms, ("group", "dp"))
+    summed = axis_by_axis(gate_terms, "dp", "group")
     gate_grad = (1.0 - gate_tanh * gate_tanh) * summed / math.sqrt(total_tokens)
     return (
         cross_output,

time: 362 us -> 196 us (0.54)
  blocking collectives: 278 us -> 113 us
    psum x1 -> x2, blocking collectives: 255 us -> 89 us  [the longest x1 70.2 us: axis_by_axis(): inner = lax.psum(value_2, inner_axis)]
  transfers between devices with their start and end apart: 2 -> 2, of which waited for: 0 -> 0; matrix products, arithmetic and copies ran while one was open for 9% -> 16% of each run, Pallas kernels for 0% -> 0%
where the time goes in v1:
time: 196 us
  blocking collectives  113 us (58%)
  matrix products  36.8 us (19%)
  other arithmetic  22.9 us (12%)
  local copies, waits for them, and re-layouts  18.3 us (9%)
  starting transfers between devices  3.38 us (2%)
    psum x1, blocking collectives, axis_by_axis(): inner = lax.psum(value_2, inner_axis)  70.2 us
    dot_general x18, matrix products, product(): return jnp.einsum(form, left, right, preferred_element_type=jnp.float32)  36.8 us
    psum x1, blocking collectives, axis_by_axis(): return lax.psum(inner, outer_axis)  18.8 us
    psum x1, blocking collectives, shards(): square_sum = lax.psum(jnp.sum(floats * floats, axis=(3, 4)), 'tensor')  13.6 us
    psum x1, blocking collectives, shards(): lax.psum(jnp.sum(gain_grad * scaled, axis=(3, 4)), 'tensor') / full_width  10.1 us
    unnamed x66, local copies, waits for them, and re-layouts  8.56 us
    unnamed x3, other arithmetic  4.53 us
  transfers between devices with their start and end apart: 2, of which 0 were waited for; matrix products, arithmetic and copies ran while one was open for 16% of the time, Pallas kernels for 0%

profile of v1, /device:TPU:2, one launch (start us, length us, event | category | flops | bytes accessed | tf_op | source)
XLA Modules:
  0.0 195.8 jit_solution(18369152454907057955)
XLA Ops:
  0.6 1.5 fusion.4
  2.2 2.8 %convert_bitcast_fusion = f32[64,8,8,128]{3,1,2,0:T(8,128)} fusion(bf16[512,1024]{1,0:T(8,128)(2,1)} %param.11), kind=kLoop, calls=%fused_computation.8 | loop fusion | flops 524288 | bytes 3145728
  5.0 13.6 %psum.28 = f32[2,2,128]{2,1,0:T(2,128)S(1)} all-reduce(f32[2,2,128]{2,1,0:T(2,128)S(1)} %bitcast.184), channel_id=1, replica_groups=mesh['group'=4,'dp'=32,'tensor'=4] {'tensor'}, use_global_device_ids=true, to_apply=%region_1.0 | all-reduce | flops 512 | bytes 4096 | tf_op jit(solution)/shard_map/psum | solution.py:102
  18.7 2.1 %copy.109 = f32[64,8,8,128]{3,2,1,0:T(8,128)S(1)} copy(f32[64,8,8,128]{3,1,2,0:T(8,128)} %convert_bitcast_fusion) | data formatting | bytes 4194304
  22.5 2.4 %fusion.6 = (bf16[2,2,128,8,128]{4,2,3,1,0:T(8,128)(2,1)S(1)}, f32[2,2,8,128,128]{3,4,2,1,0:T(8,128)}) fusion(f32[2,2,128,8,128]{4,3,2,1,0:T(8,128)S(1)} %bitcast.148, f32[2,2,8,128]{3,2,1,0:T(8,128)S(1)} %get-tuple-element.26, f32[2,2,8,128,192]{3,4,2,1,0:T(8,128)S(1)} %get-tuple-element.27, bf16[2,2,64,8,128]{4,2,3,1,0:T(8,128)(2,1)S(1)} %broadcast_in_dim.103, ...), kind=kOutput, calls=%fused_computation.14 | convolution fusion | flops 207880192 | bytes 9977856 | tf_op jit(solution)/shard_map/cjhqk,cjkhd->cjqhd/dot_general | solution.py:26
  27.2 2.1 %collective-permute-start = (bf16[256,8,128]{2,0,1:T(8,128)(2,1)}, bf16[256,8,128]{2,0,1:T(8,128)(2,1)}, u32[]{:S(2)}, u32[]{:S(2)}) collective-permute-start(bf16[256,8,128]{2,0,1:T(8,128)(2,1)} %copy.79), channel_id=1, source_target_pairs={{0,4},{4,8},{8,12},{12,16},{16,20},{20,24},{24,28},{28,32},{32,36}... | collective-permute-start | bytes 1572872 | tf_op jit(solution)/shard_map/ppermute | solution.py:22
  32.5 1.9 copy.82
  40.4 5.0 %multiply_reduce_fusion.1 = (f32[8]{0:T(128)}, f32[2,64,8]{1,2,0:T(8,128)}, bf16[2,64,8,128]{3,1,2,0:T(8,128)(2,1)}) fusion(f32[2,64,8,128]{3,2,1,0:T(8,128)} %bitcast.171, f32[8]{0:T(128)} %tanh.3, pred[2]{0:T(512)(128)(4,1)} %get-tuple-element.21, bf16[2,256,8,128]{3,2,1,0:T(8,128)(2,1)S(1)} %bitcast.155, f32[2,8,64]{2,1,0:T(8,128)S(1)} %get-tuple-element.30, ...), kind=kOutput, calls=%fused_computation.63 | convolution fusion | flops 69075192 | bytes 2891842 | tf_op jit(solution)/shard_map/bhrm,bmhd->brhd/dot_general | solution.py:26
  45.4 2.0 %fusion.13 = bf16[2,8,64,256]{3,2,1,0:T(8,128)(2,1)S(1)} fusion(bf16[2,256,8,128]{3,2,1,0:T(8,128)(2,1)S(1)} %bitcast.156, f32[2,8,64]{2,1,0:T(8,128)} %bitcast.186, f32[2,8,64,256]{3,2,1,0:T(8,128)} %get-tuple-element.31, f32[2,8,64]{2,1,0:T(8,128)S(1)} %get-tuple-element.30, f32[2,64,8,128]{3,2,1,0:T(8,128)} %bitcast.172, f32[8]{0:T(128)} %tanh.3, ...), kind=kOutput, calls=%fused_computation.30 | convolution fusion | flops 68812800 | bytes 3153954 | tf_op jit(solution)/shard_map/brhd,bmhd->bhrm/dot_general | solution.py:26
  48.4 1.9 fusion.41
  52.5 6.2 %add_bitcast_fusion.1 = f32[2,256,8,128]{1,3,2,0:T(8,128)} fusion(f32[2,8,128,256]{3,2,1,0:T(8,128)} %fusion.41, f32[2,64,8,128]{3,2,1,0:T(8,128)} %bitcast.173, f32[8]{0:T(128)S(1)} %copy-done.14, pred[2]{0:T(512)(128)(4,1)S(1)} %copy-done.16, f32[2,8,64]{2,1,0:T(8,128)S(1)} %get-tuple-element.30, f32[2,8,64,256]{3,2,1,0:T(8,128)} %copy-done.3), kind=kOutput, calls=%fused_computation.18 | convolution fusion | flops 68814080 | bytes 5771298 | tf_op jit(solution)/shard_map/bhrm,brhd->bmhd/dot_general | solution.py:26
  58.6 1.4 fusion.21
  60.9 2.8 %multiply_reduce_fusion.3 = (f32[8]{0:T(128)S(1)}, f32[64,8]{0,1:T(8,128)S(1)}, f32[1,64,8,128]{3,1,2,0:T(8,128)}) fusion(f32[1,64,8,128]{3,2,1,0:T(8,128)S(1)} %bitcast.179, f32[8]{0:T(128)S(1)} %copy-done.14, pred[]{:T(512)S(6)} %and.13, bf16[256,8,128]{2,0,1:T(8,128)(2,1)} %collective-permute-done, f32[8,64]{1,0:T(8,128)S(1)} %get-tuple-element.32, ...), kind=kOutput, calls=%fused_computation.82 | convolution fusion | flops 34406648 | bytes 1577025 | tf_op jit(solution)/shard_map/bhrm,bmhd->brhd/dot_general | solution.py:26
  63.7 1.6 fusion.24
  66.7 3.4 %fusion.17 = bf16[256,8,128]{0,2,1:T(8,128)(2,1)} fusion(f32[8,128,256]{2,1,0:T(8,128)} %fusion.45, f32[8,8,8,128]{3,2,1,0:T(8,128)} %get-tuple-element.24, f32[8]{0:T(128)S(1)} %copy-done.14, pred[]{:T(512)S(6)} %and.13, f32[8,64]{1,0:T(8,128)S(1)} %get-tuple-element.32, f32[8,64,256]{2,1,0:T(8,128)S(1)} %fusion.21), kind=kOutput, calls=%fused_computation.34 | convolution fusion | flops 34669312 | bytes 2361377 | tf_op jit(solution)/shard_map/bhrm,brhd->bmhd/dot_general | solution.py:26
  71.4 70.2 %psum.30 = f32[8]{0:T(128)S(1)} all-reduce(f32[8]{0:T(128)S(1)} %add.81), channel_id=1, replica_groups=mesh['group'=4,'dp'=32,'tensor'=4] {'dp'}, use_global_device_ids=true, to_apply=%region_15.16 | all-reduce | flops 8 | bytes 64 | tf_op jit(solution)/shard_map/psum | solution.py:15
  142.6 18.8 %psum.31 = f32[8]{0:T(128)S(1)} all-reduce(f32[8]{0:T(128)S(1)} %psum.30), channel_id=1, replica_groups=mesh['group'=4,'dp'=32,'tensor'=4] {'group'}, use_global_device_ids=true, to_apply=%region_16.17 | all-reduce | flops 8 | bytes 64 | tf_op jit(solution)/shard_map/psum | solution.py:16
  164.4 2.3 %fusion.28 = f32[2,256,8,128]{1,3,2,0:T(8,128)} fusion(f32[2,256,8,128]{1,3,2,0:T(8,128)} %add_bitcast_fusion.1, bf16[256,8,128]{0,2,1:T(8,128)(2,1)S(1)} %collective-permute-done.1), kind=kLoop, calls=%fused_computation.54 | loop fusion | flops 524288 | bytes 2621440 | tf_op jit(solution)/shard_map/scatter-add | solution.py:141
  166.8 3.0 %copy.96 = f32[2,256,8,128]{3,2,1,0:T(8,128)} copy(f32[2,256,8,128]{1,3,2,0:T(8,128)} %fusion.28) | data formatting | bytes 4194304 | tf_op jit(solution)/shard_map/scatter-add | solution.py:141
  169.8 1.9 convert_element_type.156
  172.0 2.3 %fusion.7 = f32[2,2,128,8]{2,3,1,0:T(8,128)S(1)} fusion(f32[2,2,8,128,128]{3,4,2,1,0:T(8,128)} %get-tuple-element.29, f32[2,2,128,8,128]{4,3,2,1,0:T(8,128)S(1)} %bitcast.153), kind=kLoop, calls=%fused_computation.15 | loop fusion | flops 1044480 | bytes 4210688 | tf_op jit(solution)/shard_map/reduce_sum | solution.py:48
  177.0 2.6 %multiply_reduce_fusion = (f32[2,2,128]{2,1,0:T(2,128)S(1)}, f32[2,2,128,8,128]{4,2,3,1,0:T(8,128)}) fusion(f32[2,2,128,8,128]{4,3,2,1,0:T(8,128)S(1)} %bitcast.149, f32[2,2,128]{2,1,0:T(2,128)S(1)} %add_rsqrt_fusion, f32[8,128]{1,0:T(8,128)S(1)} %bitcast.182, f32[2,2,192,8,128]{4,2,3,1,0:T(8,128)S(1)} %add_bitcast_fusion, ...), kind=kOutput, calls=%fused_computation.17 | convolution fusion | flops 207093248 | bytes 9445376 | tf_op jit(solution)/shard_map/cjhqk,cjkhd->cjqhd/dot_general | solution.py:26
  180.6 10.1 %psum.29 = f32[2,2,128]{2,1,0:T(2,128)S(1)} all-reduce(f32[2,2,128]{2,1,0:T(2,128)S(1)} %get-tuple-element.35), channel_id=1, replica_groups=mesh['group'=4,'dp'=32,'tensor'=4] {'tensor'}, use_global_device_ids=true, to_apply=%region_12.13 | all-reduce | flops 512 | bytes 4096 | tf_op jit(solution)/shard_map/psum | solution.py:157
  190.7 3.1 %add_convert_fusion = bf16[2,2,128,8,128]{4,2,3,1,0:T(8,128)(2,1)S(1)} fusion(f32[2,2,128,8,128]{4,2,3,1,0:T(8,128)} %get-tuple-element.36, f32[2,2,128,8,128]{4,3,2,1,0:T(8,128)} %bitcast.152, f32[2,2,128,8,128]{4,3,2,1,0:T(8,128)S(1)} %bitcast.150, f32[2,2,128]{2,1,0:T(2,128)S(1)} %broadcast_multiply_fusion, f32[2,2,128]{2,1,0:T(2,128)S(1)} %add_rsqrt_fusion), kind=kLoop, calls=%fused_computation.16 | loop fusion | flops 3145728 | bytes 7344128 | tf_op jit(solution)/shard_map/convert_element_type | solution.py:166
  (113 shorter events, 29.0 us)
Async XLA Ops:
  0.6 18.0 %copy-start.10 = (bf16[128,1024]{1,0:T(8,128)(2,1)S(1)}, bf16[128,1024]{1,0:T(8,128)(2,1)}, u32[]{:S(2)}) copy-start(bf16[128,1024]{1,0:T(8,128)(2,1)} %param.10) | copy-start | bytes 786436
  18.7 2.1 %copy-start.13 = (f32[1024]{0:T(1024)S(1)}, f32[1024]{0:T(1024)}, u32[]{:S(2)}) copy-start(f32[1024]{0:T(1024)} %param.13) | copy-start | bytes 12292
  22.4 2.6 %copy-start.21 = (f32[2,2,8,128,192]{3,4,2,1,0:T(8,128)}, f32[2,2,8,128,192]{3,4,2,1,0:T(8,128)S(1)}, u32[]{:S(2)}) copy-start(f32[2,2,8,128,192]{3,4,2,1,0:T(8,128)S(1)} %get-tuple-element.27) | copy-start | bytes 9437188
  22.4 2.6 %copy-start.23 = (f32[2,2,8,128]{3,2,1,0:T(8,128)}, f32[2,2,8,128]{3,2,1,0:T(8,128)S(1)}, u32[]{:S(2)}) copy-start(f32[2,2,8,128]{3,2,1,0:T(8,128)S(1)} %get-tuple-element.26) | copy-start | bytes 49156
  24.9 4.4 %copy-start.15 = (s32[1,64]{1,0:T(1,128)S(1)}, s32[1,64]{1,0:T(1,128)}, u32[]{:S(2)}) copy-start(s32[1,64]{1,0:T(1,128)} %param.12) | copy-start | bytes 772
  24.9 6.8 %copy-start.9 = (bf16[128,1024]{1,0:T(8,128)(2,1)S(1)}, bf16[128,1024]{1,0:T(8,128)(2,1)}, u32[]{:S(2)}) copy-start(bf16[128,1024]{1,0:T(8,128)(2,1)} %param.9) | copy-start | bytes 786436
  25.0 6.9 %copy-start.8 = (bf16[128,1024]{1,0:T(8,128)(2,1)S(1)}, bf16[128,1024]{1,0:T(8,128)(2,1)}, u32[]{:S(2)}) copy-start(bf16[128,1024]{1,0:T(8,128)(2,1)} %param.15) | copy-start | bytes 786436
  26.3 8.2 %copy-start.17 = (f32[8]{0:T(128)S(1)}, f32[8]{0:T(128)}, u32[]{:S(2)}) copy-start(f32[8]{0:T(128)} %param.14) | copy-start | bytes 100
  27.2 31.4 %collective-permute-start = (bf16[256,8,128]{2,0,1:T(8,128)(2,1)}, bf16[256,8,128]{2,0,1:T(8,128)(2,1)}, u32[]{:S(2)}, u32[]{:S(2)}) collective-permute-start(bf16[256,8,128]{2,0,1:T(8,128)(2,1)} %copy.79), channel_id=1, source_target_pairs={{0,4},{4,8},{8,12},{12,16},{16,20},{20,24},{24,28},{28,32},{32,36}... | collective-permute-start | bytes 1572872 | tf_op jit(solution)/shard_map/ppermute | solution.py:22
  48.4 1.9 slice-start
  48.4 3.4 %copy-start.7 = (bf16[2,64,8,128]{3,1,2,0:T(8,128)(2,1)S(1)}, bf16[2,64,8,128]{3,1,2,0:T(8,128)(2,1)}, u32[]{:S(2)}) copy-start(bf16[2,64,8,128]{3,1,2,0:T(8,128)(2,1)} %fusion.26) | copy-start | bytes 786436
  50.3 1.8 copy-start.12
  50.3 2.1 %copy-start.20 = (pred[2]{0:T(512)(128)(4,1)S(1)}, pred[2]{0:T(512)(128)(4,1)}, u32[]{:S(2)}) copy-start(pred[2]{0:T(512)(128)(4,1)} %iota_compare_fusion.1) | copy-start | bytes 10
  50.3 2.1 %copy-start.14 = (f32[8]{0:T(128)S(1)}, f32[8]{0:T(128)}, u32[]{:S(2)}) copy-start(f32[8]{0:T(128)} %tanh.3) | copy-start | bytes 100
  50.3 2.1 %copy-start.16 = (pred[2]{0:T(512)(128)(4,1)S(1)}, pred[2]{0:T(512)(128)(4,1)}, u32[]{:S(2)}) copy-start(pred[2]{0:T(512)(128)(4,1)} %get-tuple-element.21) | copy-start | bytes 10
  58.6 2.3 %copy-start.11 = (f32[8,8,8,128]{3,2,1,0:T(8,128)S(1)}, f32[8,8,8,128]{3,2,1,0:T(8,128)}, u32[]{:S(2)}) copy-start(f32[8,8,8,128]{3,2,1,0:T(8,128)} %copy.115) | copy-start | bytes 786436
  65.3 4.7 %copy-start.19 = (f32[8]{0:T(128)S(1)}, f32[8]{0:T(128)}, u32[]{:S(2)}) copy-start(f32[8]{0:T(128)} %get-tuple-element.17) | copy-start | bytes 100
  70.1 94.3 %collective-permute-start.1 = (bf16[256,8,128]{0,2,1:T(8,128)(2,1)}, bf16[256,8,128]{0,2,1:T(8,128)(2,1)S(1)}, u32[]{:S(2)}, u32[]{:S(2)}) collective-permute-start(bf16[256,8,128]{0,2,1:T(8,128)(2,1)} %fusion.17), channel_id=1, source_target_pairs={{4,0},{8,4},{12,8},{16,12},{20,16},{24,20},{28,24},{32,28},{36,32}... | collective-permute-start | bytes 1572872 | tf_op jit(solution)/shard_map/ppermute | solution.py:22
  141.6 22.3 %copy-start.18 = (f32[8]{0:T(128)S(1)}, f32[8]{0:T(128)}, u32[]{:S(2)}) copy-start(f32[8]{0:T(128)} %param.14) | copy-start | bytes 100
  169.8 2.2 %copy-start = (f32[2,256,8,128]{3,2,1,0:T(8,128)S(1)}, f32[2,256,8,128]{3,2,1,0:T(8,128)}, u32[]{:S(2)}) copy-start(f32[2,256,8,128]{3,2,1,0:T(8,128)} %copy.96) | copy-start | bytes 6291460
  169.8 4.6 %copy-start.22 = (f32[2,2,8,128,192]{3,4,2,1,0:T(8,128)S(1)}, f32[2,2,8,128,192]{3,4,2,1,0:T(8,128)}, u32[]{:S(2)}) copy-start(f32[2,2,8,128,192]{3,4,2,1,0:T(8,128)} %copy-done.21) | copy-start | bytes 9437188
  172.0 2.3 %copy-start.2 = (bf16[2,2,128,8,128]{4,2,3,1,0:T(8,128)(2,1)S(1)}, bf16[2,2,128,8,128]{4,2,3,1,0:T(8,128)(2,1)}, u32[]{:S(2)}) copy-start(bf16[2,2,128,8,128]{4,2,3,1,0:T(8,128)(2,1)} %copy-done.1) | copy-start | bytes 3145732
  172.0 2.4 %copy-start.6 = (bf16[2,2,64,8,128]{4,2,3,1,0:T(8,128)(2,1)S(1)}, bf16[2,2,64,8,128]{4,2,3,1,0:T(8,128)(2,1)}, u32[]{:S(2)}) copy-start(bf16[2,2,64,8,128]{4,2,3,1,0:T(8,128)(2,1)} %copy-done.5) | copy-start | bytes 1572868
  172.0 2.4 %copy-start.24 = (f32[2,2,8,128]{3,2,1,0:T(8,128)S(1)}, f32[2,2,8,128]{3,2,1,0:T(8,128)}, u32[]{:S(2)}) copy-start(f32[2,2,8,128]{3,2,1,0:T(8,128)} %copy-done.23) | copy-start | bytes 49156
  (4 other events, 3.9 us)
